TPU v7x, 512 devices: a whole 4x4x16 slice. The times are simulated.
512 devices in a mesh: ctx: 32 (over z_lo, y), tp: 16 (over x, z_hi, core).
Axes of the slice: x: 4, y: 4, z: 16 (z_hi: 2, z_lo: 8; z = z_hi * 8 + z_lo), core: 2. Of those that a mesh axis runs over, the one named last changes fastest.
Arguments:
- queries: bfloat16 [4096, 16384], P('ctx', 'tp'), may hold values from -12 to 12
- new_kv: bfloat16 [4096, 2048], P(('ctx', 'tp')), may hold values from -5 to 5
- cache_kv: bfloat16 [4096, 2048], P(('ctx', 'tp')), may hold values from -5 to 5
- hit_tokens: int32 [32], P('ctx'), may hold values from 1 to 128, 2560 in all
- block_order: int32 [32], P('ctx'), may hold values from 0 to 31, each once
Outputs:
- attended: bfloat16 [4096, 16384], P('ctx', 'tp')
Inputs may be any that keep to these rules, and one draw needn't show every extreme that they name: Context group d holds live cache tokens in its first hit_tokens[d] of 128 slots; the counts sum to 2560. `block_order`: each block of the turn is held by exactly one context group.
All inputs are finite; a program needn't handle non-finite values.
Results may differ from a plain program's by a relative error of at most 0.0054.
Values may be sent and summed in bfloat16 or wider, within the bound.
A program may use at most 64 MiB of HBM per device.

v0:
```python
import math

import jax
import jax.numpy as jnp
from jax import lax
from jax.sharding import PartitionSpec as P

KV = 8
HD = 128


floor_value = -1e30


def absorb(carried, query_rows, key_rows, value_rows, allowed, score_scale):
    running_max, running_total, running_sum = carried
    scores = (
        jnp.einsum("krd,skd->krs", query_rows, key_rows, preferred_element_type=jnp.float32)
        * score_scale
    )
    scores = jnp.where(allowed[None], scores, floor_value)
    new_max = jnp.maximum(running_max, jnp.max(scores, axis=2))
    weights = jnp.where(allowed[None], jnp.exp(scores - new_max[:, :, None]), 0.0)
    factor = jnp.exp(running_max - new_max)
    new_total = running_total * factor + jnp.sum(weights, axis=2)
    new_sum = running_sum * factor[:, :, None] + jnp.einsum(
        "krs,skd->krd", weights.astype(jnp.bfloat16), value_rows, preferred_element_type=jnp.float32
    )
    return (new_max, new_total, new_sum)


def local(queries, new_kv, cache_kv, hit_tokens, block_order):
    tp_count = lax.axis_size("tp")
    local_heads = max(1, KV // tp_count)
    head_copies = max(1, tp_count // KV)
    token_count = queries.shape[0]
    head_count = queries.shape[1] // HD
    group_size = head_count // local_heads
    row_count = token_count * group_size
    group_cache = cache_kv.shape[0] * tp_count
    score_scale = 1.0 / math.sqrt(HD)
    query_rows = queries.reshape(token_count, local_heads, group_size, HD).transpose(1, 0, 2, 3)
    query_rows = query_rows.reshape(local_heads, row_count, HD)
    own_block = block_order[0]
    query_position = own_block * token_count + jnp.arange(row_count, dtype=jnp.int32) // group_size

    def spread(source):
        leading = source.shape[:-1]
        shaped = source.reshape(leading + (KV, 2 * HD))
        shaped = jnp.repeat(shaped, head_copies, axis=len(leading))
        return shaped

    def take_batch(carried, batch):
        caches, new_parts, hit_counts, block_ids = batch
        members = caches.shape[0]
        key_stack = jnp.concatenate(
            [
                caches.reshape(members * group_cache, local_heads, 2, HD),
                new_parts.reshape(members * token_count, local_heads, 2, HD),
            ],
            axis=0,
        )
        cache_live = (jnp.arange(group_cache)[None, :] < hit_counts[:, None]).reshape(
            1, members * group_cache
        )
        key_position = (
            block_ids[:, None] * token_count + jnp.arange(token_count)[None, :]
        ).reshape(members * token_count)
        new_live = key_position[None, :] <= query_position[:, None]
        allowed = jnp.concatenate(
            [jnp.broadcast_to(cache_live, (row_count, members * group_cache)), new_live], axis=1
        )
        carried = absorb(
            carried, query_rows, key_stack[:, :, 0], key_stack[:, :, 1], allowed, score_scale
        )
        return (carried, None)

    initial = (
        jnp.full((local_heads, row_count), floor_value, jnp.float32),
        jnp.zeros((local_heads, row_count), jnp.float32),
        jnp.zeros((local_heads, row_count, HD), jnp.float32),
    )
    all_cache, all_new, all_hits, all_blocks = (
        lax.all_gather(cache_kv[None], "ctx", axis=0, tiled=True),
        lax.all_gather(new_kv[None], "ctx", axis=0, tiled=True),
        lax.all_gather(hit_tokens, "ctx", axis=0, tiled=True),
        lax.all_gather(block_order, "ctx", axis=0, tiled=True),
    )
    moved_cache, moved_new = (
        lax.all_to_all(spread(all_cache), "tp", split_axis=2, concat_axis=1, tiled=True),
        lax.all_to_all(spread(all_new), "tp", split_axis=2, concat_axis=1, tiled=True),
    )
    group_count = all_cache.shape[0]
    caches = moved_cache.reshape(group_count, group_cache, local_heads, 2, HD)
    new_parts = moved_new.reshape(group_count, token_count, local_heads, 2, HD)
    carried = initial
    total_groups = caches.shape[0]
    batch_size = math.gcd(total_groups, 4)

    def regroup_batch(stacked):
        return stacked.reshape((total_groups // batch_size, batch_size) + stacked.shape[1:])

    batches = (
        regroup_batch(caches),
        regroup_batch(new_parts),
        regroup_batch(all_hits),
        regroup_batch(all_blocks),
    )
    carried, unused = lax.scan(take_batch, carried, batches)
    running_max, running_total, running_sum = carried
    attended = (running_sum / running_total[:, :, None]).astype(jnp.bfloat16)
    attended = attended.reshape(local_heads, token_count, group_size, HD).transpose(1, 0, 2, 3)
    return attended.reshape(token_count, head_count * HD)


def solution(mesh):
    in_specs = (P("ctx", "tp"), P(("ctx", "tp"), None), P(("ctx", "tp"), None), P("ctx"), P("ctx"))
    out_specs = P("ctx", "tp")
    return jax.shard_map(local, mesh=mesh, in_specs=in_specs, out_specs=out_specs, check_vma=False)
```

profile of v0, /device:TPU:1, one launch (start us, length us, event | category | flops | bytes accessed | tf_op | source)
XLA Modules:
  0.0 679.8 jit_solution(14654642081545859537)
XLA Ops:
  7.3 208.1 %all-gather.5.cloned.1.call-done = bf16[256,2048]{1,0:T(8,128)(2,1)} async-done(((bf16[8,2048]{1,0:T(8,128)(2,1)}), bf16[256,2048]{1,0:T(8,128)(2,1)}) %all-gather.5.cloned.1.call-update) | async-done | bytes 1048592 | tf_op jit(solution)/shard_map/all_gather | solution.py:84
  216.6 1.6 broadcast_in_dim.47
  218.2 76.3 %all-to-all-start = ((bf16[32,8,16,256]{3,1,0,2:T(8,128)(2,1)}), bf16[32,8,16,256]{3,1,0,2:T(8,128)(2,1)S(1)}, u32[]{:S(2)}, u32[]{:S(2)}) async-start(bf16[32,8,16,256]{3,1,0,2:T(8,128)(2,1)} %bitcast.101), calls=%async_computation | async-start | bytes 4194304 | tf_op jit(solution)/shard_map/all_to_all | solution.py:90
  295.2 201.3 %all-gather.7.cloned.1.call-done = bf16[256,2048]{1,0:T(8,128)(2,1)} async-done(((bf16[8,2048]{1,0:T(8,128)(2,1)}), bf16[256,2048]{1,0:T(8,128)(2,1)}) %all-gather.7.cloned.1.call-update) | async-done | bytes 1048592 | tf_op jit(solution)/shard_map/all_gather | solution.py:85
  497.8 1.5 broadcast_in_dim.49
  499.3 76.0 %all-to-all-start.1 = ((bf16[32,8,16,256]{3,1,0,2:T(8,128)(2,1)}), bf16[32,8,16,256]{3,1,0,2:T(8,128)(2,1)}, u32[]{:S(2)}, u32[]{:S(2)}) async-start(bf16[32,8,16,256]{3,1,0,2:T(8,128)(2,1)} %bitcast.100), calls=%async_computation.1 | async-start | bytes 4194304 | tf_op jit(solution)/shard_map/all_to_all | solution.py:91
  579.4 19.3 %all-reduce.2 = (s32[32]{0:T(128)S(1)}, s32[32]{0:T(128)S(1)}) all-reduce(s32[32]{0:T(128)S(1)} %dynamic-update-slice, s32[32]{0:T(128)S(1)} %dynamic-update-slice.1), channel_id=1, replica_groups=mesh['ctx'=32,'tp'=16] {'ctx'}, use_global_device_ids=true, to_apply=%add | all-reduce | flops 64 | bytes 512
  599.0 1.6 copy.11
  600.6 4.0 reshape_reshape.6
  604.6 6.5 all-to-all-done.1
  611.0 1.8 copy.13
  612.9 2.1 reshape_reshape.7
  615.0 57.0 %while.15 = (s32[]{:T(128)}, f32[1,1024]{1,0:T(1,128)S(1)}, f32[1,1024]{1,0:T(1,128)S(1)}, f32[1,1024,128]{2,1,0:T(8,128)S(1)}, s32[8,4]{1,0:T(8,128)S(1)}, /*in...) while((s32[]{:T(128)}, f32[1,1024]{1,0:T(1,128)S(1)}, ...), condition=%wide.region_3.4_spmd.clone, body=%wide.region_0.3_spmd.clone.sunk | while | flops 555629568 | bytes 19219708 | solution.py:109
  615.5 1.4 constant_dynamic-slice_fusion.5
  618.0 2.4 fusion.56
  620.4 1.7 fusion.58
  622.6 1.4 constant_dynamic-slice_fusion.5
  625.1 2.4 fusion.56
  627.5 1.7 fusion.58
  629.8 1.4 constant_dynamic-slice_fusion.5
  632.2 2.4 fusion.56
  634.7 1.7 fusion.58
  639.3 2.4 fusion.56
  641.8 1.7 fusion.58
  646.5 2.4 fusion.56
  648.9 1.7 fusion.58
  653.6 2.4 fusion.56
  656.0 1.7 fusion.58
  660.7 2.4 fusion.56
  663.2 1.7 fusion.58
  667.8 2.4 fusion.56
  670.3 1.7 fusion.58
  (123 shorter events, 27.7 us)
Async XLA Ops:
  6.5 208.8 %all-gather.5.cloned.1.call-start = ((), (), s32[]{:S(2)}) async-start(), calls=%async_computation.2 | async-start | bytes 1081344 | tf_op jit(solution)/shard_map/all_gather | solution.py:84
  218.2 279.6 %all-to-all-start = ((bf16[32,8,16,256]{3,1,0,2:T(8,128)(2,1)}), bf16[32,8,16,256]{3,1,0,2:T(8,128)(2,1)S(1)}, u32[]{:S(2)}, u32[]{:S(2)}) async-start(bf16[32,8,16,256]{3,1,0,2:T(8,128)(2,1)} %bitcast.101), calls=%async_computation | async-start | bytes 4194304 | tf_op jit(solution)/shard_map/all_to_all | solution.py:90
  294.4 202.0 %all-gather.7.cloned.1.call-start = ((), (), s32[]{:S(2)}) async-start(), calls=%async_computation.3 | async-start | bytes 1081344 | tf_op jit(solution)/shard_map/all_gather | solution.py:85
  497.7 101.1 %copy-start = (bf16[128,1024]{1,0:T(8,128)(2,1)S(1)}, bf16[128,1024]{1,0:T(8,128)(2,1)}, u32[]{:S(2)}) copy-start(bf16[128,1024]{1,0:T(8,128)(2,1)} %param.7) | copy-start | bytes 786436
  499.3 111.8 %all-to-all-start.1 = ((bf16[32,8,16,256]{3,1,0,2:T(8,128)(2,1)}), bf16[32,8,16,256]{3,1,0,2:T(8,128)(2,1)}, u32[]{:S(2)}, u32[]{:S(2)}) async-start(bf16[32,8,16,256]{3,1,0,2:T(8,128)(2,1)} %bitcast.100), calls=%async_computation.1 | async-start | bytes 4194304 | tf_op jit(solution)/shard_map/all_to_all | solution.py:91
Sparse Core Ops, SparseCore 0:
  9.4 205.8 all-gather.4
  297.4 199.0 all-gather.6
where the time goes:
time: 685 us; the launch traced here: 680 us
  waiting for transfers between devices  417 us (61%)
  starting transfers between devices  152 us (22%)
  local copies, waits for them, and re-layouts  31 us (5%)
  other arithmetic  24 us (4%)
  matrix products  20.6 us (3%)
  blocking collectives  19.3 us (3%)
  between operations  14.8 us (2%)
    all_gather x1, waiting for transfers between devices, local(): lax.all_gather(cache_kv[None], 'ctx', axis=0, tiled=True)  208 us
    all_gather x1, waiting for transfers between devices, local(): lax.all_gather(new_kv[None], 'ctx', axis=0, tiled=True)  201 us
    all_to_all x1, starting transfers between devices, local(): lax.all_to_all(spread(all_cache), 'tp', split_axis=2, concat_axis=1, tile...  76.3 us
    all_to_all x1, starting transfers between devices, local(): lax.all_to_all(spread(all_new), 'tp', split_axis=2, concat_axis=1, tiled=...  76 us
    reduce_sum x8, other arithmetic, absorb(): new_total = running_total * factor + jnp.sum(weights, axis=2)  19.4 us
    unnamed x1, blocking collectives  19.3 us
  transfers between devices with their start and end apart: 4, of which 3 were waited for; matrix products, arithmetic and copies ran while one was open for 1% of the time, Pallas kernels for 0%

commit v1 on v0

v1 whole, which is shorter than its diff:
```python
import functools
import math

import jax
import jax.numpy as jnp
from jax import lax
from jax.experimental import pallas as pl
from jax.experimental.pallas import tpu as pltpu
from jax.sharding import PartitionSpec as P

HD = 128
MESH = pl.DeviceIdType.MESH
FLOOR = -1e30
SCALE = math.log2(math.e) / math.sqrt(HD)
ROUNDS = 16
TILE = 256
DEAD = 1e9


def kernel(q_ref, new_ref, cache_ref, meta_ref, o_ref, raw, kv, meta, qs, acc, top, tot,
           a2a_send, a2a_recv, meta_send, meta_recv, zs, ys, ss, rs):
    ctx, tp = lax.axis_index("ctx"), lax.axis_index("tp")
    lane, y = ctx // 4, ctx % 4
    x, half, core = tp // 4, (tp // 2) % 2, tp % 2
    quad, place = half * 2 + lane // 4, lane % 4
    next_quad = half * 2 + 1 - lane // 4

    def at(x_=None, y_=None, quad_=None, place_=None, core_=None):
        x_ = x if x_ is None else x_
        y_ = y if y_ is None else y_
        quad_ = quad if quad_ is None else quad_
        place_ = place if place_ is None else place_
        core_ = core if core_ is None else core_
        return (((quad_ % 2) * 4 + place_) * 4 + y_, x_ * 4 + (quad_ // 2) * 2 + core_)

    def off(value, d):
        return (value + d) % 4

    barrier = pltpu.get_barrier_semaphore()

    def greet(device):
        pl.semaphore_signal(barrier, inc=1, device_id=device, device_id_type=MESH)

    greet(at(quad_=3 - quad))
    for d in range(1, 4):
        greet(at(x_=off(x, d), quad_=3 - quad))
    greet(at(quad_=next_quad))
    for d in range(1, 4):
        greet(at(place_=off(place, d)))
        greet(at(x_=off(x, d)))
        greet(at(y_=off(y, d)))
    greet(at(core_=1 - core))

    raw[...] = jnp.concatenate([new_ref[...], cache_ref[...]], axis=0)
    meta[lane, pl.ds(y * 2, 2)] = meta_ref[...]
    for h in range(8):
        qs[h * 128:(h + 1) * 128] = q_ref[:, h * 128:(h + 1) * 128]
    acc[...] = jnp.zeros_like(acc)
    tot[...] = jnp.zeros_like(tot)
    top[...] = jnp.full_like(top, FLOOR)

    own_z = quad * 4 + place
    kv[own_z, core, y, x] = raw[:, pl.ds(pl.multiple_of((x * 2 + half) * 256, 256), 256)]

    pl.semaphore_wait(barrier, 15)

    def send(src, dst, s_sem, r_sem, device):
        return pltpu.make_async_remote_copy(src_ref=src, dst_ref=dst, send_sem=s_sem, recv_sem=r_sem,
                                            device_id=device, device_id_type=MESH)

    def piece(x_, half_):
        return raw.at[:, pl.ds(pl.multiple_of((x_ * 2 + half_) * 256, 256), 256)]

    def near_copy(d, x_from=None):
        x_from = x if x_from is None else x_from
        to = off(x, d)
        return send(piece(to, half), kv.at[own_z, core, y, x_from], a2a_send.at[d - 1], a2a_recv.at[d - 1], at(x_=to))

    def far_copy(d, arriving=False):
        to = off(x, d)
        z_from = (3 - quad) * 4 + place if arriving else own_z
        x_from = off(x, 4 - d) if arriving else x
        return send(piece(to, 1 - half), kv.at[z_from, core, y, x_from], a2a_send.at[d + 3], a2a_recv.at[d + 3], at(x_=to, quad_=3 - quad))

    def meta_y(d, row):
        rows = pl.ds(row * 2, 2)
        return send(meta.at[lane, rows], meta.at[lane, rows], meta_send.at[d - 1], meta_recv.at[d - 1], at(y_=off(y, d)))

    def meta_z(d, lane_, i):
        device = at(place_=off(place, d)) if d else at(quad_=next_quad)
        return send(meta.at[lane_], meta.at[lane_], meta_send.at[i], meta_recv.at[i], device)

    for d in range(1, 4):
        near_copy(d).start()
    for d in range(4):
        far_copy(d).start()
    for d in range(1, 4):
        meta_y(d, y).start()

    def unit(i):
        order = [(0, 0), (1, 0), (0, 1), (0, 2), (0, 3), (2, 0), (1, 1), (1, 2), (1, 3), (3, 0), (2, 1), (2, 2), (2, 3), (3, 1), (3, 2), (3, 3)]
        code = jnp.int32(order[0][0] * 4 + order[0][1])
        for n in range(1, ROUNDS):
            code = jnp.where(i == n, order[n][0] * 4 + order[n][1], code)
        kind, step = code // 4, code % 4
        from_quad = jnp.where(kind == 0, quad, jnp.where(kind == 1, 3 - quad, jnp.where(kind == 2, next_quad, 3 - next_quad)))
        return from_quad * 4 + off(place, step), kind, step

    def mate_copy(zz, d):
        ref = kv.at[zz, core, y]
        return send(ref, ref, zs.at[zz // 4, d], rs.at[zz, core, y], at(place_=off(place, d)))

    def quad_copy(zz):
        ref = kv.at[zz, core, y]
        return send(ref, ref, zs.at[zz // 4, 0], rs.at[zz, core, y], at(quad_=next_quad))

    def y_copy(zz, d):
        ref = kv.at[zz, core, y]
        return send(ref, ref, ys.at[zz, d - 1], rs.at[zz, core, y], at(y_=off(y, d)))

    def core_copy(zz, row):
        ref = kv.at[zz, core, row]
        return send(ref, ref, ss.at[zz, row], rs.at[zz, core, row], at(core_=1 - core))

    def arrival(zz, core_, row):
        ref = kv.at[zz, core_, row]
        return send(ref, ref, ss.at[zz, row], rs.at[zz, core_, row], at(core_=1 - core))

    def take_in(i):
        zz, kind, step = unit(i)

        @pl.when(i == 0)
        def _():
            for d in range(1, 4):
                near_copy(d, off(x, 4 - d)).wait_recv()

        @pl.when(i == 1)
        def _():
            for d in range(4):
                far_copy(d, True).wait_recv()

        @pl.when(i >= 2)
        def _():
            arrival(zz, core, y).wait_recv()

        @pl.when(jnp.logical_and(step == 0, kind < 2))
        def _():
            quad_copy(zz).start()

        @pl.when(step == 0)
        def _():
            for d in range(1, 4):
                mate_copy(zz, d).start()

        for d in (2, 1, 3):
            y_copy(zz, d).start()
        core_copy(zz, y).start()

    def along_y(i):
        zz, _, _ = unit(i)
        for d in (1, 3, 2):
            row = off(y, d)
            arrival(zz, core, row).wait_recv()
            core_copy(zz, row).start()

    own_block = meta_ref[1:2, :]
    number = lax.broadcasted_iota(jnp.int32, (1, 128), 1)
    token = lax.broadcasted_iota(jnp.int32, (128, 1), 0).astype(jnp.float32)
    query_position = own_block[:, 0:1] * 128.0 + token

    def key_positions(zz):
        lane_, half_ = zz % 8, zz // 8
        rows = meta[lane_]
        parts = []
        for part in range(4):
            core_, pair = part // 2, part % 2
            low = number < 64
            r = 4 * pair
            hits = jnp.where(low, rows[r:r + 1], rows[r + 2:r + 3])
            block = jnp.where(low, rows[r + 1:r + 2], rows[r + 3:r + 4])
            inner = number % 64
            slot = ((inner // 16) * 32 + half_ * 16 + core_ * 8 + inner % 8).astype(jnp.float32)
            cached = (inner // 8) % 2 == 1
            parts.append(jnp.where(cached, jnp.where(slot < hits, -1.0, DEAD), block * 128.0 + slot))
        return jnp.concatenate(parts, axis=1)

    def absorb(n):
        zz, _, _ = unit(n)
        for row in range(4):
            arrival(zz, 1 - core, row).wait_recv()
        block = kv[zz].reshape(512, 256)
        keys, values = block[:, :HD], block[:, HD:]
        allowed = key_positions(zz) <= query_position
        allowed = jnp.concatenate([allowed] * (TILE // 128), axis=0)

        def tile(t, carry):
            rows = pl.ds(pl.multiple_of(t * TILE, TILE), TILE)
            scores = lax.dot_general(qs[rows], keys, (((1,), (1,)), ((), ())), preferred_element_type=jnp.float32)
            scores = jnp.where(allowed, scores, FLOOR)
            pieces = [scores[:, i * 128:(i + 1) * 128] for i in range(4)]
            old = top[rows]
            new = jnp.maximum(old, jnp.max(functools.reduce(jnp.maximum, pieces), axis=1, keepdims=True))
            top[rows] = new
            factor = jnp.exp2((old - new) * SCALE)
            shift = new * SCALE
            weights = [jnp.exp2(piece * SCALE - shift) for piece in pieces]
            tot[rows] = tot[rows] * factor + functools.reduce(jnp.add, weights)
            rounded = jnp.concatenate([w.astype(jnp.bfloat16) for w in weights], axis=1)
            acc[rows] = acc[rows] * factor + jnp.dot(rounded, values, preferred_element_type=jnp.float32)
            return carry

        lax.fori_loop(0, 1024 // TILE, tile, 0)

    take_in(0)
    take_in(1)
    for d in range(1, 4):
        meta_y(d, off(y, 4 - d)).wait_recv()
    for d in range(4):
        meta_z(d, lane, 3 + d).start()
    next_lane = (next_quad % 2) * 4 + place
    meta_z(0, next_lane, 3).wait_recv()
    for d in range(1, 4):
        meta_z(d, next_lane, 6 + d).start()
    for d in range(1, 4):
        meta_z(d, (quad % 2) * 4 + off(place, 4 - d), 3 + d).wait_recv()
        meta_z(d, (next_quad % 2) * 4 + off(place, 4 - d), 6 + d).wait_recv()

    def rounds(n, carry):
        @pl.when(n < 7)
        def _():
            take_in(2 + 2 * n)
            take_in(3 + 2 * n)

        along_y(n)

        @pl.when(n >= 1)
        def _():
            absorb(n - 1)
        return carry

    lax.fori_loop(0, ROUNDS, rounds, 0)
    absorb(ROUNDS - 1)

    for h in range(8):
        rows = slice(h * 128, (h + 1) * 128)
        total = jnp.sum(tot[rows], axis=1, keepdims=True)
        o_ref[:, rows] = (acc[rows] / total).astype(jnp.bfloat16)

    for d in range(1, 4):
        near_copy(d).wait_send()
        meta_y(d, y).wait_send()
        meta_z(d, next_lane, 6 + d).wait_send()
    for d in range(4):
        far_copy(d).wait_send()
        meta_z(d, lane, 3 + d).wait_send()
    quad_copy(own_z).wait_send()
    quad_copy((3 - quad) * 4 + place).wait_send()

    def drain(n, carry):
        for d in range(1, 4):
            y_copy(n, d).wait_send()
        for row in range(4):
            core_copy(n, row).wait_send()
        return carry

    def drain_quads(n, carry):
        for d in range(1, 4):
            mate_copy(n * 4 + place, d).wait_send()
        return carry

    lax.fori_loop(0, ROUNDS, drain, 0)
    lax.fori_loop(0, 4, drain_quads, 0)


def local(queries, new_kv, cache_kv, hit_tokens, block_order):
    facts = jnp.broadcast_to(jnp.concatenate([hit_tokens, block_order])[:, None].astype(jnp.float32), (2, 128))
    vmem = pl.BlockSpec(memory_space=pltpu.VMEM)
    dma = pltpu.SemaphoreType.DMA
    return pl.pallas_call(
        kernel,
        out_shape=jax.ShapeDtypeStruct(queries.shape, jnp.bfloat16),
        in_specs=[vmem] * 4,
        out_specs=vmem,
        scratch_shapes=[
            pltpu.VMEM((16, 2048), jnp.bfloat16),
            pltpu.VMEM((16, 2, 4, 4, 16, 256), jnp.bfloat16),
            pltpu.VMEM((8, 8, 128), jnp.float32),
            pltpu.VMEM((1024, 128), jnp.bfloat16),
            pltpu.VMEM((1024, 128), jnp.float32),
            pltpu.VMEM((1024, 128), jnp.float32),
            pltpu.VMEM((1024, 128), jnp.float32),
            dma((7,)), dma((7,)), dma((10,)), dma((10,)),
            dma((4, 4)), dma((16, 3)), dma((16, 4)), dma((16, 2, 4)),
        ],
        compiler_params=pltpu.CompilerParams(collective_id=0, has_side_effects=True, vmem_limit_bytes=48 * 1024 * 1024),
        cost_estimate=pl.CostEstimate(flops=4 * 1024 * 8192 * 128, bytes_accessed=1 << 20, transcendentals=1024 * 8192),
    )(queries, new_kv, cache_kv, facts)


def solution(mesh):
    in_specs = (P("ctx", "tp"), P(("ctx", "tp"), None), P(("ctx", "tp"), None), P("ctx"), P("ctx"))
    return jax.shard_map(local, mesh=mesh, in_specs=in_specs, out_specs=P("ctx", "tp"), check_vma=False)
```

time: 685 us -> 78.8 us (0.12)
  waiting for transfers between devices: 417 us -> 0 us
  starting transfers between devices: 152 us -> 0 us
  Pallas kernels: 0 us -> 73.9 us
  local copies, waits for them, and re-layouts: 31 us -> 3.24 us
  other arithmetic: 24 us -> 0.08 us
  matrix products: 20.6 us -> 0 us
  blocking collectives: 19.3 us -> 0 us
  between operations: 14.8 us -> 1.31 us
    all_gather x2 -> x0, waiting for transfers between devices: 409 us -> none  [the longest x1 208 us: local(): lax.all_gather(cache_kv[None], 'ctx', axis=0, tiled=True)]
    all_to_all x2 -> x0, starting transfers between devices: 152 us -> none  [the longest x1 76.3 us: local(): lax.all_to_all(spread(all_cache), 'tp', split_axis=2, concat_axis=1, tile...]
    pallas_call x0 -> x1, Pallas kernels: none -> 73.9 us  [local(): pl.pallas_call(kernel, out_shape=jax.ShapeDtypeStruct(queries.shape, jnp....]
    dot_general x16 -> x0, matrix products: 20.6 us -> none  [the longest x8 13.2 us: absorb(): jnp.einsum('krs,skd->krd', weights.astype(jnp.bfloat16), value_rows, pref...]
    reduce_sum x8 -> x0, other arithmetic: 19.4 us -> none  [absorb(): new_total = running_total * factor + jnp.sum(weights, axis=2)]
    unnamed x1 -> x0, blocking collectives: 19.3 us -> none
    dynamic_slice x24 -> x0, local copies, waits for them, and re-layouts: 11.8 us -> none  [local(): carried, unused = lax.scan(take_batch, carried, batches)]
    another operation x4 -> x0, local copies, waits for them, and re-layouts: 7.01 us -> none  [the longest x2 6.07 us: regroup_batch(): stacked.reshape((total_groups // batch_size, batch_size) + stacked.shape[...]
  transfers between devices with their start and end apart: 4 -> 0, of which waited for: 3 -> 0; matrix products, arithmetic and copies ran while one was open for 1% -> 0% of each run, Pallas kernels for 0% -> 0%
where the time goes in v1:
time: 78.8 us; the launch traced here: 78.5 us
  Pallas kernels  73.9 us (94%)
  local copies, waits for them, and re-layouts  3.24 us (4%)
  between operations  1.31 us (2%)
    pallas_call x1, Pallas kernels, local(): pl.pallas_call(kernel, out_shape=jax.ShapeDtypeStruct(queries.shape, jnp....  73.9 us
    unnamed x7, local copies, waits for them, and re-layouts  3.17 us

profile of v1, /device:TPU:1, one launch (start us, length us, event | category | flops | bytes accessed | tf_op | source)
XLA Modules:
  0.0 78.5 jit_solution(1120629564997210111)
XLA Ops:
  1.3 0.1 add_convert_fusion
  1.4 0.1 broadcast_in_dim.2.meta_ref
  1.4 0.0 copy-start
  1.4 0.9 %copy-done = bf16[128,1024]{1,0:T(8,128)(2,1)S(1)} copy-done((bf16[128,1024]{1,0:T(8,128)(2,1)S(1)}, bf16[128,1024]{1,0:T(8,128)(2,1)}, u32[]{:S(2)}) %copy-start) | copy-done | bytes 262168
  2.4 0.0 copy-start.1
  2.4 0.8 copy-done.1
  3.2 0.0 copy-start.2
  3.2 0.8 copy-done.2
  3.9 73.9 %shard_map.55 = bf16[128,1024]{1,0:T(8,128)(2,1)S(1)} custom-call(bf16[128,1024]{1,0:T(8,128)(2,1)S(1)} %copy-done, bf16[8,2048]{1,0:T(8,128)(2,1)S(1)} %copy-done.1, bf16[8,2048]{1,0:T(8,128)(2,1)S(1)} %copy-done.2, f32[2,128]{1,0:T(2,128)S(1)} %broadcast_in_dim.2.meta_ref), custom_call_target="tpu_custom_call" | custom-call | flops 4294967296 | bytes 1048576 | tf_op jit(solution)/shard_map/pallas_call | solution.py:279
  77.8 0.7 copy.9
Async XLA Ops:
  1.4 1.0 %copy-start = (bf16[128,1024]{1,0:T(8,128)(2,1)S(1)}, bf16[128,1024]{1,0:T(8,128)(2,1)}, u32[]{:S(2)}) copy-start(bf16[128,1024]{1,0:T(8,128)(2,1)} %q_ref.1) | copy-start | bytes 786436
  2.4 0.8 copy-start.1
  3.2 0.8 copy-start.2

commit v2 on v1

--- a/solution.py
+++ b/solution.py
@@ -13,12 +13,12 @@
 FLOOR = -1e30
 SCALE = math.log2(math.e) / math.sqrt(HD)
 ROUNDS = 16
-TILE = 256
+TILE = 1024
 DEAD = 1e9
 
 
-def kernel(q_ref, new_ref, cache_ref, meta_ref, o_ref, raw, kv, meta, qs, acc, top, tot,
-           a2a_send, a2a_recv, meta_send, meta_recv, zs, ys, ss, rs):
+def kernel(q_ref, new_ref, cache_ref, hits_ref, block_ref, o_ref, new_rows, cache_rows, hits, block, raw, kv, meta, qs, acc, top, tot,
+           load_sem, a2a_send, a2a_recv, meta_send, meta_recv, zs, ys, ss, rs):
     ctx, tp = lax.axis_index("ctx"), lax.axis_index("tp")
     lane, y = ctx // 4, ctx % 4
     x, half, core = tp // 4, (tp // 2) % 2, tp % 2
@@ -51,14 +51,24 @@
         greet(at(y_=off(y, d)))
     greet(at(core_=1 - core))
 
-    raw[...] = jnp.concatenate([new_ref[...], cache_ref[...]], axis=0)
-    meta[lane, pl.ds(y * 2, 2)] = meta_ref[...]
-    for h in range(8):
-        qs[h * 128:(h + 1) * 128] = q_ref[:, h * 128:(h + 1) * 128]
+    loads = [
+        pltpu.make_async_copy(new_ref, new_rows, load_sem.at[0]),
+        pltpu.make_async_copy(cache_ref, cache_rows, load_sem.at[1]),
+        pltpu.make_async_copy(hits_ref, hits, load_sem.at[2]),
+        pltpu.make_async_copy(block_ref, block, load_sem.at[3]),
+    ] + [pltpu.make_async_copy(q_ref.at[:, h * 128:(h + 1) * 128], qs.at[h * 128:(h + 1) * 128], load_sem.at[4 + h]) for h in range(8)]
+    for load in loads:
+        load.start()
     acc[...] = jnp.zeros_like(acc)
     tot[...] = jnp.zeros_like(tot)
     top[...] = jnp.full_like(top, FLOOR)
-
+    for load in loads:
+        load.wait()
+
+    raw[...] = jnp.concatenate([new_rows[...], cache_rows[...]], axis=0)
+    own_block = block[0].astype(jnp.float32)
+    is_hits = lax.broadcasted_iota(jnp.int32, (2, 128), 0) == 0
+    meta[lane, pl.ds(y * 2, 2)] = jnp.where(is_hits, hits[0].astype(jnp.float32), own_block)
     own_z = quad * 4 + place
     kv[own_z, core, y, x] = raw[:, pl.ds(pl.multiple_of((x * 2 + half) * 256, 256), 256)]
 
@@ -163,10 +173,9 @@
             arrival(zz, core, row).wait_recv()
             core_copy(zz, row).start()
 
-    own_block = meta_ref[1:2, :]
     number = lax.broadcasted_iota(jnp.int32, (1, 128), 1)
     token = lax.broadcasted_iota(jnp.int32, (128, 1), 0).astype(jnp.float32)
-    query_position = own_block[:, 0:1] * 128.0 + token
+    query_position = own_block * 128.0 + token
 
     def key_positions(zz):
         lane_, half_ = zz % 8, zz // 8
@@ -211,35 +220,38 @@
 
         lax.fori_loop(0, 1024 // TILE, tile, 0)
 
-    take_in(0)
-    take_in(1)
+    def take_in_from(first, last):
+        lax.fori_loop(first, last, lambda i, carry: (take_in(i), carry)[1], 0)
+
+    next_lane = (next_quad % 2) * 4 + place
+    take_in_from(0, 6)
     for d in range(1, 4):
         meta_y(d, off(y, 4 - d)).wait_recv()
     for d in range(4):
         meta_z(d, lane, 3 + d).start()
-    next_lane = (next_quad % 2) * 4 + place
+    along_y(0)
+    take_in_from(6, 10)
     meta_z(0, next_lane, 3).wait_recv()
     for d in range(1, 4):
         meta_z(d, next_lane, 6 + d).start()
+    along_y(1)
     for d in range(1, 4):
         meta_z(d, (quad % 2) * 4 + off(place, 4 - d), 3 + d).wait_recv()
         meta_z(d, (next_quad % 2) * 4 + off(place, 4 - d), 6 + d).wait_recv()
 
     def rounds(n, carry):
-        @pl.when(n < 7)
-        def _():
-            take_in(2 + 2 * n)
-            take_in(3 + 2 * n)
-
-        along_y(n)
-
-        @pl.when(n >= 1)
-        def _():
-            absorb(n - 1)
+        @pl.when(n < 6)
+        def _():
+            take_in(n + 10)
+
+        @pl.when(n < ROUNDS - 2)
+        def _():
+            along_y(n + 2)
+
+        absorb(n)
         return carry
 
     lax.fori_loop(0, ROUNDS, rounds, 0)
-    absorb(ROUNDS - 1)
 
     for h in range(8):
         rows = slice(h * 128, (h + 1) * 128)
@@ -273,15 +285,17 @@
 
 
 def local(queries, new_kv, cache_kv, hit_tokens, block_order):
-    facts = jnp.broadcast_to(jnp.concatenate([hit_tokens, block_order])[:, None].astype(jnp.float32), (2, 128))
-    vmem = pl.BlockSpec(memory_space=pltpu.VMEM)
     dma = pltpu.SemaphoreType.DMA
     return pl.pallas_call(
         kernel,
         out_shape=jax.ShapeDtypeStruct(queries.shape, jnp.bfloat16),
-        in_specs=[vmem] * 4,
-        out_specs=vmem,
+        in_specs=[pl.BlockSpec(memory_space=pltpu.HBM)] * 5,
+        out_specs=pl.BlockSpec(memory_space=pltpu.VMEM),
         scratch_shapes=[
+            pltpu.VMEM((8, 2048), jnp.bfloat16),
+            pltpu.VMEM((8, 2048), jnp.bfloat16),
+            pltpu.SMEM((1,), jnp.int32),
+            pltpu.SMEM((1,), jnp.int32),
             pltpu.VMEM((16, 2048), jnp.bfloat16),
             pltpu.VMEM((16, 2, 4, 4, 16, 256), jnp.bfloat16),
             pltpu.VMEM((8, 8, 128), jnp.float32),
@@ -289,12 +303,12 @@
             pltpu.VMEM((1024, 128), jnp.float32),
             pltpu.VMEM((1024, 128), jnp.float32),
             pltpu.VMEM((1024, 128), jnp.float32),
-            dma((7,)), dma((7,)), dma((10,)), dma((10,)),
+            dma((12,)), dma((7,)), dma((7,)), dma((10,)), dma((10,)),
             dma((4, 4)), dma((16, 3)), dma((16, 4)), dma((16, 2, 4)),
         ],
         compiler_params=pltpu.CompilerParams(collective_id=0, has_side_effects=True, vmem_limit_bytes=48 * 1024 * 1024),
         cost_estimate=pl.CostEstimate(flops=4 * 1024 * 8192 * 128, bytes_accessed=1 << 20, transcendentals=1024 * 8192),
-    )(queries, new_kv, cache_kv, facts)
+    )(queries, new_kv, cache_kv, hit_tokens, block_order)
 
 
 def solution(mesh):

time: 78.8 us -> 63.4 us (0.80)
  Pallas kernels: 73.9 us -> 58 us
    pallas_call x1, Pallas kernels: 73.9 us -> 58 us  [local(): pl.pallas_call(kernel, out_shape=jax.ShapeDtypeStruct(queries.shape, jnp....]
where the time goes in v2:
time: 63.4 us; the launch traced here: 62.5 us
  Pallas kernels  58 us (91%)
  local copies, waits for them, and re-layouts  3.16 us (5%)
  between operations  1.32 us (2%)
    pallas_call x1, Pallas kernels, local(): pl.pallas_call(kernel, out_shape=jax.ShapeDtypeStruct(queries.shape, jnp....  58 us
    unnamed x7, local copies, waits for them, and re-layouts  3.16 us

profile of v2, /device:TPU:1, one launch (start us, length us, event | category | flops | bytes accessed | tf_op | source)
XLA Modules:
  0.0 62.5 jit_solution(5145378335108710037)
XLA Ops:
  1.3 0.0 copy-start
  1.3 0.9 %copy-done = bf16[128,1024]{1,0:T(8,128)(2,1)S(1)} copy-done((bf16[128,1024]{1,0:T(8,128)(2,1)S(1)}, bf16[128,1024]{1,0:T(8,128)(2,1)}, u32[]{:S(2)}) %copy-start) | copy-done | bytes 262168
  2.2 0.0 copy-start.1
  2.2 0.8 %copy-done.1 = bf16[8,2048]{1,0:T(8,128)(2,1)S(1)} copy-done((bf16[8,2048]{1,0:T(8,128)(2,1)S(1)}, bf16[8,2048]{1,0:T(8,128)(2,1)}, u32[]{:S(2)}) %copy-start.1) | copy-done | bytes 32792
  3.0 0.0 copy-start.2
  3.0 0.8 %copy-done.2 = bf16[8,2048]{1,0:T(8,128)(2,1)S(1)} copy-done((bf16[8,2048]{1,0:T(8,128)(2,1)S(1)}, bf16[8,2048]{1,0:T(8,128)(2,1)}, u32[]{:S(2)}) %copy-start.2) | copy-done | bytes 32792
  3.8 58.0 %shard_map.55 = bf16[128,1024]{1,0:T(8,128)(2,1)S(1)} custom-call(bf16[128,1024]{1,0:T(8,128)(2,1)S(1)} %copy-done, bf16[8,2048]{1,0:T(8,128)(2,1)S(1)} %copy-done.1, bf16[8,2048]{1,0:T(8,128)(2,1)S(1)} %copy-done.2, s32[1]{0:T(128)S(6)} %copy.7.hits_ref, s32[1]{0:T(128)S(6)} %copy.8.block_ref), custom_call_target="tpu_custom_call" | custom-call | flops 4294967296 | bytes 1048576 | tf_op jit(solution)/shard_map/pallas_call | solution.py:289
  61.8 0.7 %copy.9 = bf16[128,1024]{1,0:T(8,128)(2,1)} copy(bf16[128,1024]{1,0:T(8,128)(2,1)S(1)} %shard_map.55) | data formatting | bytes 524288
Async XLA Ops:
  1.3 1.0 %copy-start = (bf16[128,1024]{1,0:T(8,128)(2,1)S(1)}, bf16[128,1024]{1,0:T(8,128)(2,1)}, u32[]{:S(2)}) copy-start(bf16[128,1024]{1,0:T(8,128)(2,1)} %q_ref.1) | copy-start | bytes 786436
  2.2 0.8 %copy-start.1 = (bf16[8,2048]{1,0:T(8,128)(2,1)S(1)}, bf16[8,2048]{1,0:T(8,128)(2,1)}, u32[]{:S(2)}) copy-start(bf16[8,2048]{1,0:T(8,128)(2,1)} %new_ref.1) | copy-start | bytes 98308
  3.0 0.8 %copy-start.2 = (bf16[8,2048]{1,0:T(8,128)(2,1)S(1)}, bf16[8,2048]{1,0:T(8,128)(2,1)}, u32[]{:S(2)}) copy-start(bf16[8,2048]{1,0:T(8,128)(2,1)} %cache_ref.1) | copy-start | bytes 98308

commit v3 on v2

--- a/solution.py
+++ b/solution.py
@@ -18,7 +18,7 @@
 
 
 def kernel(q_ref, new_ref, cache_ref, hits_ref, block_ref, o_ref, new_rows, cache_rows, hits, block, raw, kv, meta, qs, acc, top, tot,
-           load_sem, a2a_send, a2a_recv, meta_send, meta_recv, zs, ys, ss, rs):
+           load_sem, a2a_send, a2a_recv, meta_send, meta_recv, zs, ys, ss, z_recv, y_recv, core_recv):
     ctx, tp = lax.axis_index("ctx"), lax.axis_index("tp")
     lane, y = ctx // 4, ctx % 4
     x, half, core = tp // 4, (tp // 2) % 2, tp % 2
@@ -118,23 +118,22 @@
 
     def mate_copy(zz, d):
         ref = kv.at[zz, core, y]
-        return send(ref, ref, zs.at[zz // 4, d], rs.at[zz, core, y], at(place_=off(place, d)))
+        return send(ref, ref, zs, z_recv.at[zz], at(place_=off(place, d)))
 
     def quad_copy(zz):
         ref = kv.at[zz, core, y]
-        return send(ref, ref, zs.at[zz // 4, 0], rs.at[zz, core, y], at(quad_=next_quad))
+        return send(ref, ref, zs, z_recv.at[zz], at(quad_=next_quad))
 
     def y_copy(zz, d):
         ref = kv.at[zz, core, y]
-        return send(ref, ref, ys.at[zz, d - 1], rs.at[zz, core, y], at(y_=off(y, d)))
-
-    def core_copy(zz, row):
-        ref = kv.at[zz, core, row]
-        return send(ref, ref, ss.at[zz, row], rs.at[zz, core, row], at(core_=1 - core))
-
-    def arrival(zz, core_, row):
-        ref = kv.at[zz, core_, row]
-        return send(ref, ref, ss.at[zz, row], rs.at[zz, core_, row], at(core_=1 - core))
+        return send(ref, ref, ys, y_recv.at[zz], at(y_=off(y, d)))
+
+    def core_copy(zz):
+        ref = kv.at[zz, core]
+        return send(ref, ref, ss, core_recv.at[zz], at(core_=1 - core))
+
+    def await_bytes(ref, semaphore):
+        pltpu.make_async_copy(ref, ref, semaphore).wait()
 
     def take_in(i):
         zz, kind, step = unit(i)
@@ -151,7 +150,7 @@
 
         @pl.when(i >= 2)
         def _():
-            arrival(zz, core, y).wait_recv()
+            await_bytes(kv.at[zz, core, y], z_recv.at[zz])
 
         @pl.when(jnp.logical_and(step == 0, kind < 2))
         def _():
@@ -164,14 +163,11 @@
 
         for d in (2, 1, 3):
             y_copy(zz, d).start()
-        core_copy(zz, y).start()
 
     def along_y(i):
         zz, _, _ = unit(i)
-        for d in (1, 3, 2):
-            row = off(y, d)
-            arrival(zz, core, row).wait_recv()
-            core_copy(zz, row).start()
+        await_bytes(kv.at[zz, core, 0:3], y_recv.at[zz])
+        core_copy(zz).start()
 
     number = lax.broadcasted_iota(jnp.int32, (1, 128), 1)
     token = lax.broadcasted_iota(jnp.int32, (128, 1), 0).astype(jnp.float32)
@@ -195,8 +191,7 @@
 
     def absorb(n):
         zz, _, _ = unit(n)
-        for row in range(4):
-            arrival(zz, 1 - core, row).wait_recv()
+        await_bytes(kv.at[zz, 1 - core], core_recv.at[zz])
         block = kv[zz].reshape(512, 256)
         keys, values = block[:, :HD], block[:, HD:]
         allowed = key_positions(zz) <= query_position
@@ -220,33 +215,41 @@
 
         lax.fori_loop(0, 1024 // TILE, tile, 0)
 
+    def pick(n, table):
+        value = jnp.int32(table[0])
+        for i in range(1, len(table)):
+            if table[i] != table[i - 1]:
+                value = jnp.where(n >= i, table[i], value)
+        return value
+
     def take_in_from(first, last):
         lax.fori_loop(first, last, lambda i, carry: (take_in(i), carry)[1], 0)
 
+    def along_y_from(first, last):
+        lax.fori_loop(first, last, lambda i, carry: (along_y(i), carry)[1], 0)
+
+    taken = [6, 10, 11, 12, 13, 14, 15, 16, 16, 16, 16, 16, 16, 16, 16, 16, 16]
+    moved = [2, 3, 4, 5, 6, 7, 8, 9, 10, 11, 12, 13, 14, 15, 16, 16, 16]
     next_lane = (next_quad % 2) * 4 + place
-    take_in_from(0, 6)
+    take_in_from(0, taken[0])
     for d in range(1, 4):
         meta_y(d, off(y, 4 - d)).wait_recv()
     for d in range(4):
         meta_z(d, lane, 3 + d).start()
-    along_y(0)
-    take_in_from(6, 10)
+    along_y_from(0, moved[0])
     meta_z(0, next_lane, 3).wait_recv()
     for d in range(1, 4):
         meta_z(d, next_lane, 6 + d).start()
-    along_y(1)
-    for d in range(1, 4):
-        meta_z(d, (quad % 2) * 4 + off(place, 4 - d), 3 + d).wait_recv()
-        meta_z(d, (next_quad % 2) * 4 + off(place, 4 - d), 6 + d).wait_recv()
 
     def rounds(n, carry):
-        @pl.when(n < 6)
-        def _():
-            take_in(n + 10)
-
-        @pl.when(n < ROUNDS - 2)
-        def _():
-            along_y(n + 2)
+        take_in_from(pick(n, taken), pick(n + 1, taken))
+        along_y_from(pick(n, moved), pick(n + 1, moved))
+
+        @pl.when(n == 2)
+        def _():
+            for d in range(1, 4):
+                meta_z(d, (quad % 2) * 4 + off(place, 4 - d), 3 + d).wait_recv()
+                meta_z(d, (next_quad % 2) * 4 + off(place, 4 - d), 6 + d).wait_recv()
 
         absorb(n)
         return carry
@@ -265,23 +268,9 @@
     for d in range(4):
         far_copy(d).wait_send()
         meta_z(d, lane, 3 + d).wait_send()
-    quad_copy(own_z).wait_send()
-    quad_copy((3 - quad) * 4 + place).wait_send()
-
-    def drain(n, carry):
-        for d in range(1, 4):
-            y_copy(n, d).wait_send()
-        for row in range(4):
-            core_copy(n, row).wait_send()
-        return carry
-
-    def drain_quads(n, carry):
-        for d in range(1, 4):
-            mate_copy(n * 4 + place, d).wait_send()
-        return carry
-
-    lax.fori_loop(0, ROUNDS, drain, 0)
-    lax.fori_loop(0, 4, drain_quads, 0)
+    await_bytes(kv.at[0:7, 0, 0:2], zs)
+    await_bytes(kv.at[0:12, 0], ys)
+    await_bytes(kv.at[:, 0], ss)
 
 
 def local(queries, new_kv, cache_kv, hit_tokens, block_order):
@@ -304,7 +293,7 @@
             pltpu.VMEM((1024, 128), jnp.float32),
             pltpu.VMEM((1024, 128), jnp.float32),
             dma((12,)), dma((7,)), dma((7,)), dma((10,)), dma((10,)),
-            dma((4, 4)), dma((16, 3)), dma((16, 4)), dma((16, 2, 4)),
+            dma, dma, dma, dma((16,)), dma((16,)), dma((16,)),
         ],
         compiler_params=pltpu.CompilerParams(collective_id=0, has_side_effects=True, vmem_limit_bytes=48 * 1024 * 1024),
         cost_estimate=pl.CostEstimate(flops=4 * 1024 * 8192 * 128, bytes_accessed=1 << 20, transcendentals=1024 * 8192),

time: 63.4 us -> 58.1 us (0.916)
  Pallas kernels: 58 us -> 53.2 us
    pallas_call x1, Pallas kernels: 58 us -> 53.2 us  [local(): pl.pallas_call(kernel, out_shape=jax.ShapeDtypeStruct(queries.shape, jnp....]
where the time goes in v3:
time: 58.1 us; the launch traced here: 57.6 us
  Pallas kernels  53.2 us (92%)
  local copies, waits for them, and re-layouts  3.16 us (5%)
  between operations  1.32 us (2%)
    pallas_call x1, Pallas kernels, local(): pl.pallas_call(kernel, out_shape=jax.ShapeDtypeStruct(queries.shape, jnp....  53.2 us
    unnamed x7, local copies, waits for them, and re-layouts  3.16 us

profile of v3, /device:TPU:1, one launch (start us, length us, event | category | flops | bytes accessed | tf_op | source)
XLA Modules:
  0.0 57.6 jit_solution(254322204214828540)
XLA Ops:
  1.3 0.0 copy-start
  1.3 0.9 %copy-done = bf16[128,1024]{1,0:T(8,128)(2,1)S(1)} copy-done((bf16[128,1024]{1,0:T(8,128)(2,1)S(1)}, bf16[128,1024]{1,0:T(8,128)(2,1)}, u32[]{:S(2)}) %copy-start) | copy-done | bytes 262168
  2.2 0.0 copy-start.1
  2.2 0.8 %copy-done.1 = bf16[8,2048]{1,0:T(8,128)(2,1)S(1)} copy-done((bf16[8,2048]{1,0:T(8,128)(2,1)S(1)}, bf16[8,2048]{1,0:T(8,128)(2,1)}, u32[]{:S(2)}) %copy-start.1) | copy-done | bytes 32792
  3.0 0.0 copy-start.2
  3.0 0.8 %copy-done.2 = bf16[8,2048]{1,0:T(8,128)(2,1)S(1)} copy-done((bf16[8,2048]{1,0:T(8,128)(2,1)S(1)}, bf16[8,2048]{1,0:T(8,128)(2,1)}, u32[]{:S(2)}) %copy-start.2) | copy-done | bytes 32792
  3.8 53.2 %shard_map.55 = bf16[128,1024]{1,0:T(8,128)(2,1)S(1)} custom-call(bf16[128,1024]{1,0:T(8,128)(2,1)S(1)} %copy-done, bf16[8,2048]{1,0:T(8,128)(2,1)S(1)} %copy-done.1, bf16[8,2048]{1,0:T(8,128)(2,1)S(1)} %copy-done.2, s32[1]{0:T(128)S(6)} %copy.7.hits_ref, s32[1]{0:T(128)S(6)} %copy.8.block_ref), custom_call_target="tpu_custom_call" | custom-call | flops 4294967296 | bytes 1048576 | tf_op jit(solution)/shard_map/pallas_call | solution.py:278
  56.9 0.7 %copy.9 = bf16[128,1024]{1,0:T(8,128)(2,1)} copy(bf16[128,1024]{1,0:T(8,128)(2,1)S(1)} %shard_map.55) | data formatting | bytes 524288
Async XLA Ops:
  1.3 1.0 %copy-start = (bf16[128,1024]{1,0:T(8,128)(2,1)S(1)}, bf16[128,1024]{1,0:T(8,128)(2,1)}, u32[]{:S(2)}) copy-start(bf16[128,1024]{1,0:T(8,128)(2,1)} %q_ref.1) | copy-start | bytes 786436
  2.2 0.8 %copy-start.1 = (bf16[8,2048]{1,0:T(8,128)(2,1)S(1)}, bf16[8,2048]{1,0:T(8,128)(2,1)}, u32[]{:S(2)}) copy-start(bf16[8,2048]{1,0:T(8,128)(2,1)} %new_ref.1) | copy-start | bytes 98308
  3.0 0.8 %copy-start.2 = (bf16[8,2048]{1,0:T(8,128)(2,1)S(1)}, bf16[8,2048]{1,0:T(8,128)(2,1)}, u32[]{:S(2)}) copy-start(bf16[8,2048]{1,0:T(8,128)(2,1)} %cache_ref.1) | copy-start | bytes 98308

commit v4 on v3

--- a/solution.py
+++ b/solution.py
@@ -229,7 +229,7 @@
         lax.fori_loop(first, last, lambda i, carry: (along_y(i), carry)[1], 0)
 
     taken = [6, 10, 11, 12, 13, 14, 15, 16, 16, 16, 16, 16, 16, 16, 16, 16, 16]
-    moved = [2, 3, 4, 5, 6, 7, 8, 9, 10, 11, 12, 13, 14, 15, 16, 16, 16]
+    moved = [1, 3, 4, 5, 6, 7, 8, 9, 10, 11, 12, 13, 14, 15, 16, 16, 16]
     next_lane = (next_quad % 2) * 4 + place
     take_in_from(0, taken[0])
     for d in range(1, 4):
@@ -295,7 +295,7 @@
             dma((12,)), dma((7,)), dma((7,)), dma((10,)), dma((10,)),
             dma, dma, dma, dma((16,)), dma((16,)), dma((16,)),
         ],
-        compiler_params=pltpu.CompilerParams(collective_id=0, has_side_effects=True, vmem_limit_bytes=48 * 1024 * 1024),
+        compiler_params=pltpu.CompilerParams(collective_id=0, has_side_effects=True, vmem_limit_bytes=56 * 1024 * 1024),
         cost_estimate=pl.CostEstimate(flops=4 * 1024 * 8192 * 128, bytes_accessed=1 << 20, transcendentals=1024 * 8192),
     )(queries, new_kv, cache_kv, hit_tokens, block_order)
 

time: 58.1 us -> 57.2 us (0.985)
  local copies, waits for them, and re-layouts: 3.16 us -> 1.67 us
  Pallas kernels: 53.2 us -> 53.8 us
    unnamed x7 -> x1, local copies, waits for them, and re-layouts: 3.16 us -> 1.67 us
    pallas_call x1, Pallas kernels: 53.2 us -> 53.8 us  [local(): pl.pallas_call(kernel, out_shape=jax.ShapeDtypeStruct(queries.shape, jnp....]
where the time goes in v4:
time: 57.2 us; the launch traced here: 56.8 us
  Pallas kernels  53.8 us (94%)
  local copies, waits for them, and re-layouts  1.67 us (3%)
  between operations  1.3 us (2%)
    pallas_call x1, Pallas kernels, local(): pl.pallas_call(kernel, out_shape=jax.ShapeDtypeStruct(queries.shape, jnp....  53.8 us
    unnamed x1, local copies, waits for them, and re-layouts  1.67 us

profile of v4, /device:TPU:1, one launch (start us, length us, event | category | flops | bytes accessed | tf_op | source)
XLA Modules:
  0.0 56.8 jit_solution(132687453413087018)
XLA Ops:
  1.3 53.8 %shard_map.55 = bf16[128,1024]{1,0:T(8,128)(2,1)} custom-call(bf16[128,1024]{1,0:T(8,128)(2,1)} %q_ref.1, bf16[8,2048]{1,0:T(8,128)(2,1)} %new_ref.1, bf16[8,2048]{1,0:T(8,128)(2,1)} %cache_ref.1, s32[1]{0:T(128)S(6)} %copy.7.hits_ref, s32[1]{0:T(128)S(6)} %copy.8.block_ref), custom_call_target="tpu_custom_call" | custom-call | flops 4294967296 | bytes 1048576 | tf_op jit(solution)/shard_map/pallas_call | solution.py:278
  55.2 1.7 %copy.9 = bf16[128,1024]{1,0:T(8,128)(2,1)} copy(bf16[128,1024]{1,0:T(8,128)(2,1)} %shard_map.55) | data formatting | bytes 524288

commit v5 on v4

--- a/solution.py
+++ b/solution.py
@@ -231,11 +231,12 @@
     taken = [6, 10, 11, 12, 13, 14, 15, 16, 16, 16, 16, 16, 16, 16, 16, 16, 16]
     moved = [1, 3, 4, 5, 6, 7, 8, 9, 10, 11, 12, 13, 14, 15, 16, 16, 16]
     next_lane = (next_quad % 2) * 4 + place
-    take_in_from(0, taken[0])
+    take_in_from(0, 1)
     for d in range(1, 4):
         meta_y(d, off(y, 4 - d)).wait_recv()
     for d in range(4):
         meta_z(d, lane, 3 + d).start()
+    take_in_from(1, taken[0])
     along_y_from(0, moved[0])
     meta_z(0, next_lane, 3).wait_recv()
     for d in range(1, 4):

time: 57.2 us -> 54.8 us (0.958)
  the two profiles are of different devices: /device:TPU:1 before, /device:TPU:36 now
where the time goes in v5:
time: 54.8 us; the launch traced here: 54.6 us
  Pallas kernels  51.6 us (94%)
  local copies, waits for them, and re-layouts  1.67 us (3%)
  between operations  1.3 us (2%)
    pallas_call x1, Pallas kernels, local(): pl.pallas_call(kernel, out_shape=jax.ShapeDtypeStruct(queries.shape, jnp....  51.6 us
    unnamed x1, local copies, waits for them, and re-layouts  1.67 us

profile of v5, /device:TPU:36, one launch (start us, length us, event | category | flops | bytes accessed | tf_op | source)
XLA Modules:
  0.0 54.6 jit_solution(9122727814944333039)
XLA Ops:
  1.3 51.6 %shard_map.55 = bf16[128,1024]{1,0:T(8,128)(2,1)} custom-call(bf16[128,1024]{1,0:T(8,128)(2,1)} %q_ref.1, bf16[8,2048]{1,0:T(8,128)(2,1)} %new_ref.1, bf16[8,2048]{1,0:T(8,128)(2,1)} %cache_ref.1, s32[1]{0:T(128)S(6)} %copy.7.hits_ref, s32[1]{0:T(128)S(6)} %copy.8.block_ref), custom_call_target="tpu_custom_call" | custom-call | flops 4294967296 | bytes 1048576 | tf_op jit(solution)/shard_map/pallas_call | solution.py:279
  52.9 1.7 %copy.9 = bf16[128,1024]{1,0:T(8,128)(2,1)} copy(bf16[128,1024]{1,0:T(8,128)(2,1)} %shard_map.55) | data formatting | bytes 524288

commit v6 on v5

--- a/solution.py
+++ b/solution.py
@@ -237,10 +237,10 @@
     for d in range(4):
         meta_z(d, lane, 3 + d).start()
     take_in_from(1, taken[0])
+    meta_z(0, next_lane, 3).wait_recv()
+    for d in range(1, 4):
+        meta_z(d, next_lane, 6 + d).start()
     along_y_from(0, moved[0])
-    meta_z(0, next_lane, 3).wait_recv()
-    for d in range(1, 4):
-        meta_z(d, next_lane, 6 + d).start()
 
     def rounds(n, carry):
         take_in_from(pick(n, taken), pick(n + 1, taken))

time: 54.8 us -> 54.8 us (level)
  no operation moved by 1% of the time
where the time goes in v6:
time: 54.8 us; the launch traced here: 54.6 us
  Pallas kernels  51.6 us (94%)
  local copies, waits for them, and re-layouts  1.67 us (3%)
  between operations  1.3 us (2%)
    pallas_call x1, Pallas kernels, local(): pl.pallas_call(kernel, out_shape=jax.ShapeDtypeStruct(queries.shape, jnp....  51.6 us
    unnamed x1, local copies, waits for them, and re-layouts  1.67 us

profile of v6, /device:TPU:36, one launch (start us, length us, event | category | flops | bytes accessed | tf_op | source)
XLA Modules:
  0.0 54.6 jit_solution(2024250817454005514)
XLA Ops:
  1.3 51.6 %shard_map.55 = bf16[128,1024]{1,0:T(8,128)(2,1)} custom-call(bf16[128,1024]{1,0:T(8,128)(2,1)} %q_ref.1, bf16[8,2048]{1,0:T(8,128)(2,1)} %new_ref.1, bf16[8,2048]{1,0:T(8,128)(2,1)} %cache_ref.1, s32[1]{0:T(128)S(6)} %copy.7.hits_ref, s32[1]{0:T(128)S(6)} %copy.8.block_ref), custom_call_target="tpu_custom_call" | custom-call | flops 4294967296 | bytes 1048576 | tf_op jit(solution)/shard_map/pallas_call | solution.py:279
  52.9 1.7 %copy.9 = bf16[128,1024]{1,0:T(8,128)(2,1)} copy(bf16[128,1024]{1,0:T(8,128)(2,1)} %shard_map.55) | data formatting | bytes 524288
